TPU v7x, 512 devices: a whole 4x4x16 slice. The times are simulated.
512 devices in a mesh: dom: 64 (over x, z), col: 8 (over y, core).
Axes of the slice: x: 4, y: 4, z: 16, core: 2. Of those that a mesh axis runs over, the one named last changes fastest.
Arguments:
- tiles: bfloat16 [6144, 128, 128], P('dom'), may hold values from -0.21875 to 0.21875
- tile_rows: int32 [6144], P('dom'), may hold values from 0 to 15, as said below
- tile_srcs: int32 [6144], P('dom'), may hold values from 0 to 79, as said below
- send_rows: int32 [64, 64], P('dom'), may hold values from 0 to 15
- basis: bfloat16 [256, 131072], P('col', 'dom')
- rotation: bfloat16 [256, 256], P(None, 'col'), may hold values from -0.375 to 0.375
Outputs:
- gram: float32 [256, 256], P(None, 'col')
- rotated: bfloat16 [256, 131072], P('col', 'dom')
Inputs may be any that keep to these rules, and one draw needn't show every extreme that they name: `tile_rows`: every one of a device's 16 row blocks holds one or more of its tiles. `tile_srcs`: a device's pool is its own 16 row blocks followed by the block received from each of the 64 devices of dom in order; each received block is named by exactly one tile of the device.
All inputs are finite; a program needn't handle non-finite values.
Results may differ from a plain program's by a relative error of at most 0.0052.
The roundings to bfloat16 on the way count: a program that leaves them out, or rounds other values in their place, can miss the bound.
Values may be sent and summed in bfloat16 or wider, within the bound.
A program may use at most 64 MiB of HBM per device.

v0:
```python
import jax
import jax.numpy as jnp
from jax import lax
from jax.sharding import PartitionSpec as P


def propagate(field, tiles, tile_rows, tile_srcs, send_rows):
    width, rows = field.shape
    tile = tiles.shape[1]
    count = rows // tile
    blocks = field.reshape(width, count, tile)
    outgoing = jnp.take(blocks, send_rows[0], axis=1)
    arrived = lax.all_to_all(outgoing, "dom", split_axis=1, concat_axis=1, tiled=True)
    pool = jnp.concatenate([blocks, arrived], axis=1)
    sources = jnp.take(pool, tile_srcs, axis=1)
    contrib = jnp.einsum("ktj,tij->kti", sources, tiles, preferred_element_type=jnp.float32)
    owner = (tile_rows[:, None] == jnp.arange(count, dtype=jnp.int32)[None, :]).astype(jnp.float32)
    summed = jnp.einsum("kti,tr->kri", contrib, owner, precision=lax.Precision.HIGHEST)
    return summed.reshape(width, rows).astype(jnp.bfloat16)


def per_device(tiles, tile_rows, tile_srcs, send_rows, basis, rotation):
    first = propagate(basis, tiles, tile_rows, tile_srcs, send_rows)
    second = propagate(first, tiles, tile_rows, tile_srcs, send_rows)
    total_rows = second.shape[1] * lax.axis_size("dom")
    whole = lax.all_gather(second, "col", axis=0, tiled=True)
    partial_value = lax.dot_general(
        whole, second, (((1,), (1,)), ((), ())), preferred_element_type=jnp.float32
    )
    gram = lax.psum(partial_value, "dom") / total_rows
    rotated = lax.dot_general(
        rotation, whole, (((0,), (0,)), ((), ())), preferred_element_type=jnp.float32
    ).astype(jnp.bfloat16)
    return (gram, rotated)


def solution(mesh):
    return jax.shard_map(
        per_device,
        mesh=mesh,
        in_specs=(
            P("dom", None, None),
            P("dom"),
            P("dom"),
            P("dom", None),
            P("col", "dom"),
            P(None, "col"),
        ),
        out_specs=(P(None, "col"), P("col", "dom")),
        check_vma=False,
    )
```

profile of v0, /device:TPU:16, one launch (start us, length us, event | category | flops | bytes accessed | tf_op | source)
XLA Modules:
  0.0 435.3 jit_solution(9607265423307653355)
XLA Ops:
  7.2 0.0 copy-start
  7.2 0.8 compare_and_fusion.1
  8.0 0.8 compare_select_fusion.1
  8.8 0.9 copy_bitcast_fusion.1
  9.7 0.0 copy-start.3
  9.7 1.4 gather_fusion
  11.2 2.0 select_bitcast_fusion.1
  13.1 18.8 %all-to-all-start = ((bf16[32,64,128]{2,0,1:T(8,128)(2,1)}), bf16[32,64,128]{2,0,1:T(8,128)(2,1)}, u32[]{:S(2)}, u32[]{:S(2)}) async-start(bf16[32,64,128]{2,0,1:T(8,128)(2,1)} %select_bitcast_fusion.1), calls=%async_computation | async-start | bytes 1048576 | tf_op jit(solution)/shard_map/all_to_all | solution.py:13
  32.0 0.0 all-gather.2.cloned.1.call-start
  32.0 0.0 copy-done.3
  32.1 31.5 %all-to-all-done = bf16[32,64,128]{2,0,1:T(8,128)(2,1)} async-done(((bf16[32,64,128]{2,0,1:T(8,128)(2,1)}), bf16[32,64,128]{2,0,1:T(8,128)(2,1)}, u32[]{:S(2)}, u32[]{:S(2)}) %all-to-all-start) | async-done | bytes 524320 | tf_op jit(solution)/shard_map/all_to_all | solution.py:13
  63.5 2.0 pad_maximum_fusion
  65.5 2.7 gather_fusion.1
  68.1 0.0 copy-done
  68.1 0.0 copy-start.2
  68.1 2.9 convolution_bitcast_fusion.1
  71.1 0.0 copy-done.2
  71.1 1.5 fusion.11
  72.6 1.4 gather_fusion.2
  74.0 1.2 select_bitcast_fusion
  75.2 37.4 %all_to_all.10 = bf16[32,64,128]{2,0,1:T(8,128)(2,1)S(1)} all-to-all(bf16[32,64,128]{2,0,1:T(8,128)(2,1)S(1)} %select_bitcast_fusion), channel_id=1, replica_groups=mesh['dom'=64,'col'=8] {'dom'}, dimensions={1} | all-to-all | bytes 1048576 | tf_op jit(solution)/shard_map/all_to_all | solution.py:13
  112.6 0.9 pad_maximum_fusion.1
  113.6 2.7 gather_fusion.3
  116.2 2.9 convolution_bitcast_fusion
  119.1 0.0 copy-start.1
  119.1 1.5 fusion.8
  120.7 0.7 copy.31
  121.3 0.0 all-gather.2.cloned.1.call-update
  121.4 22.9 %all-gather.2.cloned.1.call-done = bf16[256,2048]{1,0:T(8,128)(2,1)} async-done(((bf16[32,2048]{1,0:T(8,128)(2,1)}), bf16[256,2048]{1,0:T(8,128)(2,1)}) %all-gather.2.cloned.1.call-update) | async-done | bytes 1048592 | tf_op jit(solution)/shard_map/all_gather | solution.py:26
  144.3 1.6 fusion.29
  145.9 279.8 %psum.7 = f32[256,32]{0,1:T(8,128)S(1)} all-reduce(f32[256,32]{0,1:T(8,128)S(1)} %fusion.29), channel_id=1, replica_groups=mesh['dom'=64,'col'=8] {'dom'}, use_global_device_ids=true, to_apply=%region_0.3 | all-reduce | flops 8192 | bytes 65536 | tf_op jit(solution)/shard_map/psum | solution.py:30
  425.7 0.6 broadcast_multiply_fusion
  426.3 0.0 copy-done.1
  426.3 2.2 fusion
  (5 shorter events, 0.1 us)
Async XLA Ops:
  7.2 61.0 %copy-start = (bf16[96,128,128]{2,1,0:T(8,128)(2,1)S(1)}, bf16[96,128,128]{2,1,0:T(8,128)(2,1)}, u32[]{:S(2)}) copy-start(bf16[96,128,128]{2,1,0:T(8,128)(2,1)} %param.10) | copy-start | bytes 9437188
  9.7 22.3 %copy-start.3 = (s32[96]{0:T(128)S(1)}, s32[96]{0:T(128)}, u32[]{:S(2)}) copy-start(s32[96]{0:T(128)} %param.12) | copy-start | bytes 1156
  13.1 50.4 %all-to-all-start = ((bf16[32,64,128]{2,0,1:T(8,128)(2,1)}), bf16[32,64,128]{2,0,1:T(8,128)(2,1)}, u32[]{:S(2)}, u32[]{:S(2)}) async-start(bf16[32,64,128]{2,0,1:T(8,128)(2,1)} %select_bitcast_fusion.1), calls=%async_computation | async-start | bytes 1048576 | tf_op jit(solution)/shard_map/all_to_all | solution.py:13
  32.0 112.3 %all-gather.2.cloned.1.call-start = ((), (), s32[]{:S(2)}) async-start(), calls=%async_computation.2 | async-start | bytes 1179648 | tf_op jit(solution)/shard_map/all_gather | solution.py:26
  68.1 2.9 copy-start.2
  119.1 307.2 %copy-start.1 = (bf16[256,32]{0,1:T(8,128)(2,1)S(1)}, bf16[256,32]{0,1:T(8,128)(2,1)}, u32[]{:S(2)}) copy-start(bf16[256,32]{0,1:T(8,128)(2,1)} %param.15) | copy-start | bytes 49156
Sparse Core Ops, SparseCore 0:
  121.5 22.7 all-gather.1
where the time goes:
time: 436 us; the launch traced here: 435 us
  blocking collectives  317 us (73%)
  waiting for transfers between devices  54.4 us (12%)
  starting transfers between devices  18.9 us (4%)
  between operations  14.1 us (3%)
  matrix products  12.7 us (3%)
  local copies, waits for them, and re-layouts  9.84 us (2%)
  other arithmetic  8.26 us (2%)
    psum x1, blocking collectives, per_device(): gram = lax.psum(partial_value, 'dom') / total_rows  280 us
    all_to_all x1, blocking collectives, propagate(): lax.all_to_all(outgoing, 'dom', split_axis=1, concat_axis=1, tiled=True)  37.4 us
    all_to_all x1, waiting for transfers between devices, propagate(): lax.all_to_all(outgoing, 'dom', split_axis=1, concat_axis=1, tiled=True)  31.5 us
    all_gather x1, waiting for transfers between devices, per_device(): whole = lax.all_gather(second, 'col', axis=0, tiled=True)  22.9 us
    all_to_all x1, starting transfers between devices, propagate(): lax.all_to_all(outgoing, 'dom', split_axis=1, concat_axis=1, tiled=True)  18.8 us
  transfers between devices with their start and end apart: 2, of which 2 were waited for; matrix products, arithmetic and copies ran while one was open for 0% of the time, Pallas kernels for 0%

commit v1 on v0

v1 whole, which is shorter than its diff:
```python
import jax
import jax.numpy as jnp
from jax import lax
from jax.experimental import pallas as pl
from jax.experimental.pallas import tpu as pltpu
from jax.sharding import PartitionSpec as P

MESH = pl.DeviceIdType.MESH
TILE = 128
RB = 16
TPD = 96
WIDTH = 32
K = 256
ROWS = RB * TILE
NX, NZ = 4, 16
NDOM = NX * NZ
NY, NCORE = 4, 2
NCOL = NY * NCORE
OWN = TPD - NDOM
GROUP = 4


def dom_at(me, i, sign):
    x, z = me // NZ, me % NZ
    kk = NZ - 1 - i // NX
    dz = jnp.where(kk % 2 == 1, (kk + 1) // 2, NZ - (kk + 1) // 2)
    dx = NX - 1 - i % NX
    return ((x + sign * dx + NX) % NX) * NZ + (z + sign * dz + NZ) % NZ


def loop(lo, hi, body):
    def step(i, carry):
        body(i)
        return carry

    lax.fori_loop(lo, hi, step, 0)


def build_tables(rows, srcs, tab):
    tab[...] = jnp.zeros_like(tab)
    at = lax.broadcasted_iota(jnp.int32, (TPD, TPD), 0)
    other = lax.broadcasted_iota(jnp.int32, (TPD, TPD), 1)
    rows_l = jnp.broadcast_to(rows[...], (TPD, TPD))
    srcs_l = jnp.broadcast_to(srcs[...], (TPD, TPD))

    def along(value):
        return jnp.sum(value, axis=1, keepdims=True)

    def across(value):
        return jnp.sum(value, axis=0, keepdims=True)

    one = jnp.ones((TPD, TPD), jnp.int32)
    zero = jnp.zeros((TPD, TPD), jnp.int32)
    rows_c = along(jnp.where(at == other, rows_l, zero))
    srcs_c = along(jnp.where(at == other, srcs_l, zero))
    earlier = other < at
    own_rank = along(jnp.where(jnp.logical_and(earlier, srcs_l < RB), one, zero))
    slot = jnp.where(srcs_c < RB, jnp.minimum(NDOM + own_rank, TPD - 1), srcs_c - RB)
    same_before = along(jnp.where(jnp.logical_and(rows_l == rows_c, earlier), one, zero))
    place = along(jnp.where(rows_l < rows_c, one, zero)) + same_before
    keep = jnp.minimum(same_before, 1)
    slot_here = slot == other
    place_here = place == other
    def put(n, most, value):
        tab[n : n + 1, 0:TPD] = jnp.minimum(across(value), most)

    put(0, TPD - 1, jnp.where(slot_here, at, zero))
    put(1, RB - 1, jnp.where(slot_here, jnp.broadcast_to(jnp.minimum(srcs_c, RB - 1), (TPD, TPD)), zero))
    put(2, TPD - 1, jnp.where(place_here, jnp.broadcast_to(slot, (TPD, TPD)), zero))
    put(3, 1, jnp.where(place_here, jnp.broadcast_to(keep, (TPD, TPD)), zero))
    upto = across(jnp.where(rows_c <= other, one, zero))
    tab[4:5, 0:TPD] = jnp.maximum(upto - 1, 0)


def kernel(
    tiles_h, rows_h, srcs_h, send_h, basis_h, rot_h,
    gram_ref, out_ref,
    tiles, rows, srcs, send_rows, basis, rot, tab, tabs,
    field, sbuf, rbuf, prods, sums, whole,
    gsend, grecv, gx, gfin,
    in_sem, ssem, rsem, row_sem, csend, crecv, gs1, gr1, gs2, gr2, gs3, gr3,
):
    me, mc = lax.axis_index("dom"), lax.axis_index("col")
    x, z = me // NZ, me % NZ
    y, core = mc // NCORE, mc % NCORE
    bar = pltpu.get_barrier_semaphore()

    loads = [
        pltpu.make_async_copy(src, dst, in_sem.at[n])
        for n, (src, dst) in enumerate(
            ((basis_h, basis), (send_h, send_rows), (rows_h, rows), (srcs_h, srcs), (tiles_h, tiles), (rot_h, rot))
        )
    ]
    for load in loads:
        load.start()

    def z_peer(d):
        return x * NZ + (z + d) % NZ

    def x_peer(d):
        return ((x + d) % NX) * NZ + z

    def y_peer(d):
        return ((y + d) % NY) * NCORE + core

    sibling = y * NCORE + 1 - core

    def greet(sem, **where):
        pl.semaphore_signal(sem, inc=1, device_id=where, device_id_type=MESH)

    for d in range(1, NX):
        greet(bar, dom=x_peer(d))
    loop(1, NZ, lambda d: greet(bar, dom=z_peer(d)))
    for d in range(1, NY):
        greet(bar, col=y_peer(d))
    greet(bar, col=sibling)

    for n in range(2):
        loads[n].wait()
    for r in range(RB):
        field[r] = basis[:, r * TILE : (r + 1) * TILE]

    pl.semaphore_wait(bar, NX - 1 + NZ - 1 + NY)
    for d in range(1, NX):
        greet(row_sem, dom=x_peer(d))
    pl.semaphore_wait(row_sem, NX - 1)

    def halo(p, peer, slot):
        return pltpu.make_async_remote_copy(
            src_ref=sbuf.at[p, peer], dst_ref=rbuf.at[p, slot],
            send_sem=ssem.at[p, peer], recv_sem=rsem.at[p, slot],
            device_id={"dom": peer}, device_id_type=MESH,
        )

    def product(block, tile):
        return lax.dot_general(block, tile, (((1,), (1,)), ((), ())), preferred_element_type=jnp.float32)

    for p in range(2):

        def send(i):
            peer = dom_at(me, i, 1)
            sbuf[p, peer] = field[send_rows[0, peer]]
            halo(p, peer, me).start()

        loop(0, NDOM - 1, send)
        rbuf[p, me] = field[send_rows[0, me]]

        if p == 0:
            for n in range(2, 5):
                loads[n].wait()
            build_tables(rows, srcs, tab)
            to_smem = pltpu.make_async_copy(tab, tabs, in_sem.at[6])
            to_smem.start()
            to_smem.wait()

        def own(g):
            for u in range(GROUP):
                s = NDOM + g * GROUP + u
                prods[s] = product(field[tabs[1, s]], tiles[tabs[0, s]])

        loop(0, OWN // GROUP, own)

        def received(g):
            origins = [dom_at(me, g * GROUP + u, -1) for u in range(GROUP)]
            for origin in origins:
                halo(p, origin, origin).wait_recv()
            for origin in origins:
                prods[origin] = product(rbuf[p, origin], tiles[tabs[0, origin]])

        loop(0, NDOM // GROUP - 1, received)
        last = [dom_at(me, NDOM - GROUP + u, -1) for u in range(GROUP)]
        for origin in last[:-1]:
            halo(p, origin, origin).wait_recv()
        for origin in last:
            prods[origin] = product(rbuf[p, origin], tiles[tabs[0, origin]])

        def running(g, acc):
            for u in range(GROUP):
                s = g * GROUP + u
                acc = jnp.where(tabs[3, s] > 0, acc, 0.0) + prods[tabs[2, s]]
                sums[s] = acc
            return acc

        lax.fori_loop(0, TPD // GROUP, running, jnp.zeros((WIDTH, TILE), jnp.float32))
        for r in range(RB):
            block = sums[tabs[4, r]].astype(jnp.bfloat16)
            if p == 0:
                field[r] = block
            else:
                whole[pl.ds(pl.multiple_of(mc * WIDTH, WIDTH), WIDTH), r * TILE : (r + 1) * TILE] = block

    def part(owner):
        return whole.at[pl.ds(pl.multiple_of(owner * WIDTH, WIDTH), WIDTH)]

    def pass_on(owner, to, n):
        return pltpu.make_async_remote_copy(
            src_ref=part(owner), dst_ref=part(owner), send_sem=csend.at[n], recv_sem=crecv.at[n],
            device_id={"col": to}, device_id_type=MESH,
        )

    outward = [pass_on(mc, y_peer(d), d) for d in (2, 1, 3)] + [pass_on(mc, sibling, 0)]
    for copy in outward:
        copy.start()
    loads[5].wait()
    rotation = rot[...].T
    onward = []
    for d in (1, 3, 2):
        origin = y_peer(NY - d)
        pass_on(origin, mc, d).wait_recv()
        copy = pass_on(origin, sibling, NY + d)
        copy.start()
        onward.append(copy)
    pass_on(sibling, mc, 0).wait_recv()
    for d in (1, 3, 2):
        pass_on(((y + NY - d) % NY) * NCORE + 1 - core, mc, NY + d).wait_recv()

    gram = lax.dot_general(
        part(mc)[...], whole[...], (((1,), (1,)), ((), ())), preferred_element_type=jnp.float32
    ) * (1.0 / (ROWS * NDOM))
    for k in range(NZ):
        gsend[k, 0:2] = gram[2 * k : 2 * k + 2, 0:TILE]
        gsend[k, 2:4] = gram[2 * k : 2 * k + 2, TILE : 2 * TILE]

    def gram_out(d, sign):
        to = (z + sign * d + NZ) % NZ
        return pltpu.make_async_remote_copy(
            src_ref=gsend.at[to], dst_ref=grecv.at[z], send_sem=gs1.at[d], recv_sem=gr1.at[d],
            device_id={"dom": x * NZ + to}, device_id_type=MESH,
        )

    loop(1, NZ, lambda d: gram_out(d, 1).start())
    grecv[z] = gsend[z]

    def rotate(c):
        cols = pl.ds(pl.multiple_of(c * 512, 512), 512)
        out_ref[:, cols] = jnp.dot(rotation, whole[:, cols], preferred_element_type=jnp.float32).astype(jnp.bfloat16)

    loop(0, ROWS // 512, rotate)

    loop(1, NZ, lambda d: gram_out(d, -1).wait_recv())
    total = grecv[0]
    for k in range(1, NZ):
        total = total + grecv[k]
    gx[x] = total

    def gram_x(d):
        return pltpu.make_async_remote_copy(
            src_ref=gx.at[x], dst_ref=gx.at[x], send_sem=gs2.at[d], recv_sem=gr2.at[d],
            device_id={"dom": x_peer(d)}, device_id_type=MESH,
        )

    def gram_x_from(d):
        origin = (x + NX - d) % NX
        return pltpu.make_async_remote_copy(
            src_ref=gx.at[origin], dst_ref=gx.at[origin], send_sem=gs2.at[d], recv_sem=gr2.at[d],
            device_id={"dom": x_peer(d)}, device_id_type=MESH,
        )

    for d in range(1, NX):
        gram_x(d).start()
    for d in range(1, NX):
        gram_x_from(d).wait_recv()
    gfin[z] = ((gx[0] + gx[1]) + gx[2]) + gx[3]

    def gram_back(owner, d):
        return pltpu.make_async_remote_copy(
            src_ref=gfin.at[owner], dst_ref=gfin.at[owner], send_sem=gs3.at[d], recv_sem=gr3.at[d],
            device_id={"dom": z_peer(d)}, device_id_type=MESH,
        )

    loop(1, NZ, lambda d: gram_back(z, d).start())
    loop(1, NZ, lambda d: gram_back((z + NZ - d) % NZ, d).wait_recv())
    for half in range(2):
        rows_of = jnp.concatenate([gfin[k, 2 * half : 2 * half + 2] for k in range(NZ)], axis=0)
        gram_ref[half * TILE : (half + 1) * TILE, :] = rows_of.T

    for p in range(2):
        loop(0, NDOM - 1, lambda i: halo(p, dom_at(me, i, 1), me).wait_send())
    for copy in outward + onward:
        copy.wait_send()
    loop(1, NZ, lambda d: gram_out(d, 1).wait_send())
    for d in range(1, NX):
        gram_x(d).wait_send()
    loop(1, NZ, lambda d: gram_back(z, d).wait_send())


def per_device(tiles, tile_rows, tile_srcs, send_rows, basis, rotation):
    any_space = pl.BlockSpec(memory_space=pl.ANY)
    vmem = pl.BlockSpec(memory_space=pltpu.VMEM)
    dma = pltpu.SemaphoreType.DMA
    return pl.pallas_call(
        kernel,
        out_shape=(
            jax.ShapeDtypeStruct((K, WIDTH), jnp.float32),
            jax.ShapeDtypeStruct((WIDTH, ROWS), jnp.bfloat16),
        ),
        in_specs=[any_space] * 6,
        out_specs=(vmem, vmem),
        scratch_shapes=[
            pltpu.VMEM((TPD, TILE, TILE), jnp.bfloat16),
            pltpu.VMEM((1, TPD), jnp.int32),
            pltpu.VMEM((1, TPD), jnp.int32),
            pltpu.SMEM((1, NDOM), jnp.int32),
            pltpu.VMEM((WIDTH, ROWS), jnp.bfloat16),
            pltpu.VMEM((K, WIDTH), jnp.bfloat16),
            pltpu.VMEM((8, 128), jnp.int32),
            pltpu.SMEM((8, 128), jnp.int32),
            pltpu.VMEM((RB, WIDTH, TILE), jnp.bfloat16),
            pltpu.VMEM((2, NDOM, WIDTH, TILE), jnp.bfloat16),
            pltpu.VMEM((2, NDOM, WIDTH, TILE), jnp.bfloat16),
            pltpu.VMEM((TPD, WIDTH, TILE), jnp.float32),
            pltpu.VMEM((TPD, WIDTH, TILE), jnp.float32),
            pltpu.VMEM((K, ROWS), jnp.bfloat16),
            pltpu.VMEM((NZ, 4, TILE), jnp.float32),
            pltpu.VMEM((NZ, 4, TILE), jnp.float32),
            pltpu.VMEM((NX, 4, TILE), jnp.float32),
            pltpu.VMEM((NZ, 4, TILE), jnp.float32),
            dma((7,)),
            dma((2, NDOM)),
            dma((2, NDOM)),
            pltpu.SemaphoreType.REGULAR,
            dma((2 * NY,)),
            dma((2 * NY,)),
            dma((NZ,)),
            dma((NZ,)),
            dma((NX,)),
            dma((NX,)),
            dma((NZ,)),
            dma((NZ,)),
        ],
        compiler_params=pltpu.CompilerParams(collective_id=0, has_side_effects=True, vmem_limit_bytes=56 << 20),
        cost_estimate=pl.CostEstimate(flops=300_000_000, bytes_accessed=4 << 20, transcendentals=0),
    )(tiles, tile_rows.reshape(1, TPD), tile_srcs.reshape(1, TPD), send_rows, basis, rotation)


def solution(mesh):
    return jax.shard_map(
        per_device,
        mesh=mesh,
        in_specs=(
            P("dom", None, None),
            P("dom"),
            P("dom"),
            P("dom", None),
            P("col", "dom"),
            P(None, "col"),
        ),
        out_specs=(P(None, "col"), P("col", "dom")),
        check_vma=False,
    )
```

time: 436 us -> 111 us (0.25)
  the two profiles are of different devices: /device:TPU:16 before, /device:TPU:1 now
where the time goes in v1:
time: 111 us; the launch traced here: 110 us
  Pallas kernels  105 us (95%)
  local copies, waits for them, and re-layouts  4.61 us (4%)
    pallas_call x1, Pallas kernels, per_device(): pl.pallas_call(kernel, out_shape=(jax.ShapeDtypeStruct((K, WIDTH), jnp.fl...  105 us
    unnamed x2, local copies, waits for them, and re-layouts  3.02 us

profile of v1, /device:TPU:1, one launch (start us, length us, event | category | flops | bytes accessed | tf_op | source)
XLA Modules:
  0.0 109.9 jit_solution(6137102223244678778)
XLA Ops:
  0.6 1.5 %copy.8.rot_h = bf16[256,32]{1,0:T(8,128)(2,1)} copy(bf16[256,32]{0,1:T(8,128)(2,1)} %param.11) | data formatting | bytes 32768 | tf_op args[5]
  2.1 104.6 %shard_map.77 = (f32[256,32]{1,0:T(8,128)}, bf16[32,2048]{1,0:T(8,128)(2,1)}) custom-call(bf16[96,128,128]{2,1,0:T(8,128)(2,1)} %tiles_h.1, s32[1,96]{1,0:T(1,128)} %bitcast.2, s32[1,96]{1,0:T(1,128)} %bitcast.3, s32[1,64]{1,0:T(1,128)} %send_h.1, bf16[32,2048]{1,0:T(8,128)(2,1)} %basis_h.1, bf16[256,32]{1,0:T(8,128)(2,1)} %copy.8.rot_h), custom_call_target="tpu_custom_call" | custom-call | flops 300000000 | bytes 4194304 | tf_op jit(solution)/shard_map/pallas_call | solution.py:291
  106.7 1.6 %copy.9 = f32[256,32]{0,1:T(8,128)} copy(f32[256,32]{1,0:T(8,128)} %get-tuple-element.2) | data formatting | bytes 65536 | tf_op jit(solution)/shard_map/pallas_call | solution.py:291
  108.3 1.6 %copy.11 = bf16[32,2048]{1,0:T(8,128)(2,1)} copy(bf16[32,2048]{1,0:T(8,128)(2,1)} %get-tuple-element.7) | data formatting | bytes 262144

commit v2 on v1

v2 whole, which is shorter than its diff:
```python
import jax
import jax.numpy as jnp
from jax import lax
from jax.experimental import pallas as pl
from jax.experimental.pallas import tpu as pltpu
from jax.sharding import PartitionSpec as P

MESH = pl.DeviceIdType.MESH
TILE = 128
RB = 16
TPD = 96
WIDTH = 32
K = 256
ROWS = RB * TILE
NX, NZ = 4, 16
NDOM = NX * NZ
NY, NCORE = 4, 2
NCOL = NY * NCORE
OWN = TPD - NDOM
GROUP = 4
HALF = NZ // 2
HALVES = 2
PART = WIDTH // HALVES
CHUNK = WIDTH // NX


def loop(lo, hi, body):
    def step(i, carry):
        body(i)
        return carry

    lax.fori_loop(lo, hi, step, 0)


def build_tables(rows, srcs, tab):
    tab[...] = jnp.zeros_like(tab)
    at = lax.broadcasted_iota(jnp.int32, (TPD, TPD), 0)
    other = lax.broadcasted_iota(jnp.int32, (TPD, TPD), 1)
    rows_l = jnp.broadcast_to(rows[...], (TPD, TPD))
    srcs_l = jnp.broadcast_to(srcs[...], (TPD, TPD))

    def along(value):
        return jnp.sum(value, axis=1, keepdims=True)

    def across(value):
        return jnp.sum(value, axis=0, keepdims=True)

    one = jnp.ones((TPD, TPD), jnp.int32)
    zero = jnp.zeros((TPD, TPD), jnp.int32)
    rows_c = along(jnp.where(at == other, rows_l, zero))
    srcs_c = along(jnp.where(at == other, srcs_l, zero))
    earlier = other < at
    own_rank = along(jnp.where(jnp.logical_and(earlier, srcs_l < RB), one, zero))
    slot = jnp.where(srcs_c < RB, jnp.minimum(NDOM + own_rank, TPD - 1), srcs_c - RB)
    same_before = along(jnp.where(jnp.logical_and(rows_l == rows_c, earlier), one, zero))
    place = along(jnp.where(rows_l < rows_c, one, zero)) + same_before
    keep = jnp.minimum(same_before, 1)
    slot_here = slot == other
    place_here = place == other
    def put(n, most, value):
        tab[n : n + 1, 0:TPD] = jnp.minimum(across(value), most)

    put(0, TPD - 1, jnp.where(slot_here, at, zero))
    put(1, RB - 1, jnp.where(slot_here, jnp.broadcast_to(jnp.minimum(srcs_c, RB - 1), (TPD, TPD)), zero))
    put(2, TPD - 1, jnp.where(place_here, jnp.broadcast_to(slot, (TPD, TPD)), zero))
    put(3, 1, jnp.where(place_here, jnp.broadcast_to(keep, (TPD, TPD)), zero))
    upto = across(jnp.where(rows_c <= other, one, zero))
    tab[4:5, 0:TPD] = jnp.maximum(upto - 1, 0)


def kernel(
    tiles_h, rows_h, srcs_h, send_h, basis_h, rot_h,
    gram_ref, out_ref,
    tiles, rows, srcs, send_rows, basis, rot, tab, tabs,
    field, sbuf, rbuf, prods, sums, whole,
    gpart, gx, gsum, gz,
    in_sem, ssem, rsem, csend, crecv, gs1, gr1, gs2, gr2, gs3, gr3,
):
    me, mc = lax.axis_index("dom"), lax.axis_index("col")
    x, z = lax.div(me, NZ), lax.rem(me, NZ)
    y, core = lax.div(mc, NCORE), lax.rem(mc, NCORE)
    lines_to = [lax.rem(x + dx, NX) * NZ for dx in range(NX)]
    lines_from = [lax.rem(x + NX - dx, NX) * NZ for dx in range(NX)]

    def targets(j):
        ahead = (lax.rem(z + HALF + j, NZ), lax.rem(z + HALF - 1 - j, NZ))
        return [line + at for at in ahead for line in lines_to[::-1]]

    def origins(j):
        behind = (lax.rem(z + HALF - j, NZ), lax.rem(z + HALF + 1 + j, NZ))
        return [line + at for at in behind for line in lines_from[::-1]]

    def over_peers(body):
        loop(0, HALF - 1, lambda j: body(j, 2 * NX))
        body(HALF - 1, 2 * NX - 1)
    bar = pltpu.get_barrier_semaphore()

    loads = [
        pltpu.make_async_copy(src, dst, in_sem.at[n])
        for n, (src, dst) in enumerate(
            ((basis_h, basis), (send_h, send_rows), (rows_h, rows), (srcs_h, srcs), (tiles_h, tiles), (rot_h, rot))
        )
    ]
    for load in loads:
        load.start()

    def y_peer(d):
        return ((y + d) % NY) * NCORE + core

    sibling = y * NCORE + 1 - core

    def greet(**where):
        pl.semaphore_signal(bar, inc=1, device_id=where, device_id_type=MESH)

    def greet_peers(j, most):
        for peer in targets(j)[:most]:
            greet(dom=peer)

    over_peers(greet_peers)
    for d in range(1, NY):
        greet(col=y_peer(d))
    greet(col=sibling)

    for n in range(2):
        loads[n].wait()
    for h in range(HALVES):
        for r in range(RB):
            field[h, r] = basis[h * PART : (h + 1) * PART, r * TILE : (r + 1) * TILE]

    pl.semaphore_wait(bar, NDOM - 1 + NY)

    def halo(p, h, peer, slot):
        return pltpu.make_async_remote_copy(
            src_ref=sbuf.at[p, h, peer], dst_ref=rbuf.at[p, h, slot],
            send_sem=ssem.at[p, h, peer], recv_sem=rsem.at[p, h, slot],
            device_id={"dom": peer}, device_id_type=MESH,
        )

    def product(block, tile):
        return lax.dot_general(block, tile, (((1,), (1,)), ((), ())), preferred_element_type=jnp.float32)

    def send(p, h):
        def some(j, most):
            peers = targets(j)
            for peer in peers[:most]:
                sbuf[p, h, peer] = field[h, send_rows[0, peer]]
            for peer in peers[:most]:
                halo(p, h, peer, me).start()

        over_peers(some)
        rbuf[p, h, me] = field[h, send_rows[0, me]]

    def send_ended(p, h):
        def some(j, most):
            for peer in targets(j)[:most]:
                halo(p, h, peer, me).wait_send()

        over_peers(some)

    def own(h):
        def group(g):
            for u in range(GROUP):
                s = NDOM + g * GROUP + u
                prods[h, s] = product(field[h, tabs[1, s]], tiles[tabs[0, s]])

        loop(0, OWN // GROUP, group)

    def receive(p, h, first, past):
        def take(j, waits):
            peers = origins(j)
            for peer in peers[:waits]:
                halo(p, h, peer, peer).wait_recv()
            for peer in peers:
                prods[h, peer] = product(rbuf[p, h, peer], tiles[tabs[0, peer]])

        loop(first, min(past, HALF - 1), lambda j: take(j, 2 * NX))
        if past == HALF:
            take(HALF - 1, 2 * NX - 1)

    def add_up(h):
        def running(g, acc):
            for u in range(GROUP):
                s = g * GROUP + u
                acc = jnp.where(tabs[3, s] > 0, acc, 0.0) + prods[h, tabs[2, s]]
                sums[s] = acc
            return acc

        lax.fori_loop(0, TPD // GROUP, running, jnp.zeros((PART, TILE), jnp.float32))
        return [sums[tabs[4, r]].astype(jnp.bfloat16) for r in range(RB)]

    def part(owner, h):
        return whole.at[pl.ds(pl.multiple_of(owner * WIDTH + h * PART, PART), PART)]

    def pass_on(owner, h, to, n):
        return pltpu.make_async_remote_copy(
            src_ref=part(owner, h), dst_ref=part(owner, h), send_sem=csend.at[h, n], recv_sem=crecv.at[h, n],
            device_id={"col": to}, device_id_type=MESH,
        )

    sent = []

    def begin(copy):
        copy.start()
        sent.append(copy)

    def spread_out(h):
        for d in (2, 1, 3):
            begin(pass_on(mc, h, y_peer(d), d))
        begin(pass_on(mc, h, sibling, 0))

    def hand_over(h):
        for d in (1, 3, 2):
            origin = y_peer(NY - d)
            pass_on(origin, h, mc, d).wait_recv()
            begin(pass_on(origin, h, sibling, NY + d))

    def gathered(h):
        pass_on(sibling, h, mc, 0).wait_recv()
        for d in (1, 3, 2):
            pass_on(((y + NY - d) % NY) * NCORE + 1 - core, h, mc, NY + d).wait_recv()

    def first_done(h):
        for r, block in enumerate(add_up(h)):
            field[h, r] = block

    def second_done(h):
        mine = pl.ds(pl.multiple_of(mc * WIDTH + h * PART, PART), PART)
        for r, block in enumerate(add_up(h)):
            whole[mine, r * TILE : (r + 1) * TILE] = block

    for h in range(HALVES):
        send(0, h)
    for n in range(2, 5):
        loads[n].wait()
    build_tables(rows, srcs, tab)
    to_smem = pltpu.make_async_copy(tab, tabs, in_sem.at[6])
    to_smem.start()
    to_smem.wait()
    for h in range(HALVES):
        own(h)
    for h in range(HALVES):
        receive(0, h, 0, HALF)
        first_done(h)
        send(1, h)
        own(h)
    for h in range(HALVES):
        receive(1, h, 0, HALF - 2)
        if h > 0:
            hand_over(h - 1)
        receive(1, h, HALF - 2, HALF)
        second_done(h)
        spread_out(h)
    loads[5].wait()
    for h in range(HALVES - 1):
        gathered(h)
    hand_over(HALVES - 1)
    gathered(HALVES - 1)

    mine = pl.ds(pl.multiple_of(mc * WIDTH, WIDTH), WIDTH)
    gram = lax.dot_general(
        whole[mine, :], whole[...], (((1,), (1,)), ((), ())), preferred_element_type=jnp.float32
    ) * (1.0 / (ROWS * NDOM))
    for k in range(NX):
        gpart[k] = gram[k * CHUNK : (k + 1) * CHUNK, :]

    def x_scatter(d, sign):
        to = (x + sign * d + NX) % NX
        return pltpu.make_async_remote_copy(
            src_ref=gpart.at[to], dst_ref=gx.at[x], send_sem=gs1.at[d], recv_sem=gr1.at[d],
            device_id={"dom": to * NZ + z}, device_id_type=MESH,
        )

    for d in range(1, NX):
        x_scatter(d, 1).start()
    gx[x] = gpart[x]
    for d in range(1, NX):
        x_scatter(d, -1).wait_recv()
    gz[z] = ((gx[0] + gx[1]) + gx[2]) + gx[3]

    def z_share(owner, d):
        return pltpu.make_async_remote_copy(
            src_ref=gz.at[owner], dst_ref=gz.at[owner], send_sem=gs2.at[d], recv_sem=gr2.at[d],
            device_id={"dom": x * NZ + (z + d) % NZ}, device_id_type=MESH,
        )

    z_order = sorted(range(1, NZ), key=lambda d: -min(d, NZ - d))
    for d in z_order:
        z_share(z, d).start()

    def rotate(c):
        cols = pl.ds(pl.multiple_of(c * 512, 512), 512)
        out_ref[:, cols] = jnp.dot(rot[...], whole[:, cols], preferred_element_type=jnp.float32).astype(jnp.bfloat16)

    loop(0, ROWS // 512, rotate)
    for d in z_order:
        z_share((z + NZ - d) % NZ, d).wait_recv()
    total = gz[0]
    for k in range(1, NZ):
        total = total + gz[k]
    gsum[x] = total

    def x_share(owner, d):
        return pltpu.make_async_remote_copy(
            src_ref=gsum.at[owner], dst_ref=gsum.at[owner], send_sem=gs3.at[d], recv_sem=gr3.at[d],
            device_id={"dom": ((x + d) % NX) * NZ + z}, device_id_type=MESH,
        )

    for d in range(1, NX):
        x_share(x, d).start()
    for p in range(2):
        for h in range(HALVES):
            send_ended(p, h)
    for copy in sent:
        copy.wait_send()
    for d in range(1, NX):
        x_scatter(d, 1).wait_send()
    for d in range(1, NZ):
        z_share(z, d).wait_send()
    for d in range(1, NX):
        x_share((x + NX - d) % NX, d).wait_recv()
    for k in range(NX):
        gram_ref[k * CHUNK : (k + 1) * CHUNK, :] = gsum[k]
    for d in range(1, NX):
        x_share(x, d).wait_send()


def per_device(tiles, tile_rows, tile_srcs, send_rows, basis, rotation):
    any_space = pl.BlockSpec(memory_space=pl.ANY)
    vmem = pl.BlockSpec(memory_space=pltpu.VMEM)
    dma = pltpu.SemaphoreType.DMA
    gram, rotated = pl.pallas_call(
        kernel,
        out_shape=(
            jax.ShapeDtypeStruct((WIDTH, K), jnp.float32),
            jax.ShapeDtypeStruct((WIDTH, ROWS), jnp.bfloat16),
        ),
        in_specs=[any_space] * 6,
        out_specs=(vmem, vmem),
        scratch_shapes=[
            pltpu.VMEM((TPD, TILE, TILE), jnp.bfloat16),
            pltpu.VMEM((1, TPD), jnp.int32),
            pltpu.VMEM((1, TPD), jnp.int32),
            pltpu.SMEM((1, NDOM), jnp.int32),
            pltpu.VMEM((WIDTH, ROWS), jnp.bfloat16),
            pltpu.VMEM((WIDTH, K), jnp.bfloat16),
            pltpu.VMEM((8, 128), jnp.int32),
            pltpu.SMEM((8, 128), jnp.int32),
            pltpu.VMEM((HALVES, RB, PART, TILE), jnp.bfloat16),
            pltpu.VMEM((2, HALVES, NDOM, PART, TILE), jnp.bfloat16),
            pltpu.VMEM((2, HALVES, NDOM, PART, TILE), jnp.bfloat16),
            pltpu.VMEM((HALVES, TPD, PART, TILE), jnp.float32),
            pltpu.VMEM((TPD, PART, TILE), jnp.float32),
            pltpu.VMEM((K, ROWS), jnp.bfloat16),
            pltpu.VMEM((NX, CHUNK, K), jnp.float32),
            pltpu.VMEM((NX, CHUNK, K), jnp.float32),
            pltpu.VMEM((NX, CHUNK, K), jnp.float32),
            pltpu.VMEM((NZ, CHUNK, K), jnp.float32),
            dma((7,)),
            dma((2, HALVES, NDOM)),
            dma((2, HALVES, NDOM)),
            dma((HALVES, 2 * NY)),
            dma((HALVES, 2 * NY)),
            dma((NX,)),
            dma((NX,)),
            dma((NZ,)),
            dma((NZ,)),
            dma((NX,)),
            dma((NX,)),
        ],
        compiler_params=pltpu.CompilerParams(collective_id=0, has_side_effects=True, vmem_limit_bytes=56 << 20),
        cost_estimate=pl.CostEstimate(flops=300_000_000, bytes_accessed=4 << 20, transcendentals=0),
    )(tiles, tile_rows.reshape(1, TPD), tile_srcs.reshape(1, TPD), send_rows, basis, rotation.T)
    return gram.T, rotated


def solution(mesh):
    return jax.shard_map(
        per_device,
        mesh=mesh,
        in_specs=(
            P("dom", None, None),
            P("dom"),
            P("dom"),
            P("dom", None),
            P("col", "dom"),
            P(None, "col"),
        ),
        out_specs=(P(None, "col"), P("col", "dom")),
        check_vma=False,
    )
```

time: 111 us -> 98.1 us (0.88)
  Pallas kernels: 105 us -> 94.3 us
  local copies, waits for them, and re-layouts: 4.61 us -> 2.94 us
    pallas_call x1, Pallas kernels: 105 us -> 94.3 us  [per_device(): pl.pallas_call(kernel, out_shape=(jax.ShapeDtypeStruct((WIDTH, K), jnp.fl...]
    pallas_call x1 -> x0, local copies, waits for them, and re-layouts: 1.59 us -> none  [per_device(): pl.pallas_call(kernel, out_shape=(jax.ShapeDtypeStruct((K, WIDTH), jnp.fl...]
where the time goes in v2:
time: 98.1 us; the launch traced here: 97.8 us
  Pallas kernels  94.3 us (96%)
  local copies, waits for them, and re-layouts  2.94 us (3%)
    pallas_call x1, Pallas kernels, per_device(): pl.pallas_call(kernel, out_shape=(jax.ShapeDtypeStruct((WIDTH, K), jnp.fl...  94.3 us
    unnamed x2, local copies, waits for them, and re-layouts  2.94 us

profile of v2, /device:TPU:1, one launch (start us, length us, event | category | flops | bytes accessed | tf_op | source)
XLA Modules:
  0.0 97.8 jit_solution(18181917920848298696)
XLA Ops:
  0.6 94.3 %shard_map.77 = (f32[32,256]{1,0:T(8,128)}, bf16[32,2048]{1,0:T(8,128)(2,1)}) custom-call(bf16[96,128,128]{2,1,0:T(8,128)(2,1)} %tiles_h.1, s32[1,96]{1,0:T(1,128)} %bitcast.6, s32[1,96]{1,0:T(1,128)} %bitcast.7, s32[1,64]{1,0:T(1,128)} %send_h.1, bf16[32,2048]{1,0:T(8,128)(2,1)} %basis_h.1, bf16[32,256]{1,0:T(8,128)(2,1)} %bitcast.5), custom_call_target="tpu_custom_call" | custom-call | flops 300000000 | bytes 4194304 | tf_op jit(solution)/shard_map/pallas_call | solution.py:331
  94.9 1.4 %copy.10 = f32[256,32]{0,1:T(8,128)} copy(f32[256,32]{0,1:T(8,128)} %bitcast.4) | data formatting | bytes 65536
  96.3 1.6 %copy.11 = bf16[32,2048]{1,0:T(8,128)(2,1)} copy(bf16[32,2048]{1,0:T(8,128)(2,1)} %get-tuple-element.9) | data formatting | bytes 262144

commit v3 on v2

--- a/solution.py
+++ b/solution.py
@@ -19,6 +19,7 @@
 OWN = TPD - NDOM
 GROUP = 4
 HALF = NZ // 2
+BATCH = 2 * NX
 HALVES = 2
 PART = WIDTH // HALVES
 CHUNK = WIDTH // NX
@@ -74,7 +75,7 @@
     tiles, rows, srcs, send_rows, basis, rot, tab, tabs,
     field, sbuf, rbuf, prods, sums, whole,
     gpart, gx, gsum, gz,
-    in_sem, ssem, rsem, csend, crecv, gs1, gr1, gs2, gr2, gs3, gr3,
+    in_sem, ssem, rsem, csend, crecv, gsem,
 ):
     me, mc = lax.axis_index("dom"), lax.axis_index("col")
     x, z = lax.div(me, NZ), lax.rem(me, NZ)
@@ -91,8 +92,8 @@
         return [line + at for at in behind for line in lines_from[::-1]]
 
     def over_peers(body):
-        loop(0, HALF - 1, lambda j: body(j, 2 * NX))
-        body(HALF - 1, 2 * NX - 1)
+        loop(0, HALF - 1, lambda j: body(j, BATCH))
+        body(HALF - 1, BATCH - 1)
     bar = pltpu.get_barrier_semaphore()
 
     loads = [
@@ -129,11 +130,18 @@
 
     pl.semaphore_wait(bar, NDOM - 1 + NY)
 
-    def halo(p, h, peer, slot):
-        return pltpu.make_async_remote_copy(
-            src_ref=sbuf.at[p, h, peer], dst_ref=rbuf.at[p, h, slot],
-            send_sem=ssem.at[p, h, peer], recv_sem=rsem.at[p, h, slot],
+    def halo(p, h, j, u, peer):
+        slot = j * BATCH + u
+        return pltpu.make_async_remote_copy(
+            src_ref=sbuf.at[p, h, slot], dst_ref=rbuf.at[p, h, slot], send_sem=ssem.at[p, h], recv_sem=rsem.at[p, h, j],
             device_id={"dom": peer}, device_id_type=MESH,
+        )
+
+    def halo_batch(p, h, j, first, count):
+        slots = pl.ds(first, count)
+        return pltpu.make_async_remote_copy(
+            src_ref=sbuf.at[p, h, slots], dst_ref=rbuf.at[p, h, slots], send_sem=ssem.at[p, h], recv_sem=rsem.at[p, h, j],
+            device_id={"dom": x * NZ + lax.rem(z + 1, NZ)}, device_id_type=MESH,
         )
 
     def product(block, tile):
@@ -142,20 +150,13 @@
     def send(p, h):
         def some(j, most):
             peers = targets(j)
-            for peer in peers[:most]:
-                sbuf[p, h, peer] = field[h, send_rows[0, peer]]
-            for peer in peers[:most]:
-                halo(p, h, peer, me).start()
+            for u, peer in enumerate(peers[:most]):
+                sbuf[p, h, j * BATCH + u] = field[h, send_rows[0, peer]]
+            for u, peer in enumerate(peers[:most]):
+                halo(p, h, j, u, peer).start()
 
         over_peers(some)
-        rbuf[p, h, me] = field[h, send_rows[0, me]]
-
-    def send_ended(p, h):
-        def some(j, most):
-            for peer in targets(j)[:most]:
-                halo(p, h, peer, me).wait_send()
-
-        over_peers(some)
+        rbuf[p, h, NDOM - 1] = field[h, send_rows[0, me]]
 
     def own(h):
         def group(g):
@@ -167,15 +168,13 @@
 
     def receive(p, h, first, past):
         def take(j, waits):
-            peers = origins(j)
-            for peer in peers[:waits]:
-                halo(p, h, peer, peer).wait_recv()
-            for peer in peers:
-                prods[h, peer] = product(rbuf[p, h, peer], tiles[tabs[0, peer]])
-
-        loop(first, min(past, HALF - 1), lambda j: take(j, 2 * NX))
+            halo_batch(p, h, j, j * BATCH, waits).wait_recv()
+            for u, peer in enumerate(origins(j)):
+                prods[h, peer] = product(rbuf[p, h, j * BATCH + u], tiles[tabs[0, peer]])
+
+        loop(first, min(past, HALF - 1), lambda j: take(j, BATCH))
         if past == HALF:
-            take(HALF - 1, 2 * NX - 1)
+            take(HALF - 1, BATCH - 1)
 
     def add_up(h):
         def running(g, acc):
@@ -193,26 +192,20 @@
 
     def pass_on(owner, h, to, n):
         return pltpu.make_async_remote_copy(
-            src_ref=part(owner, h), dst_ref=part(owner, h), send_sem=csend.at[h, n], recv_sem=crecv.at[h, n],
+            src_ref=part(owner, h), dst_ref=part(owner, h), send_sem=csend.at[h], recv_sem=crecv.at[h, n],
             device_id={"col": to}, device_id_type=MESH,
         )
-
-    sent = []
-
-    def begin(copy):
-        copy.start()
-        sent.append(copy)
 
     def spread_out(h):
         for d in (2, 1, 3):
-            begin(pass_on(mc, h, y_peer(d), d))
-        begin(pass_on(mc, h, sibling, 0))
+            pass_on(mc, h, y_peer(d), d).start()
+        pass_on(mc, h, sibling, 0).start()
 
     def hand_over(h):
         for d in (1, 3, 2):
             origin = y_peer(NY - d)
             pass_on(origin, h, mc, d).wait_recv()
-            begin(pass_on(origin, h, sibling, NY + d))
+            pass_on(origin, h, sibling, NY + d).start()
 
     def gathered(h):
         pass_on(sibling, h, mc, 0).wait_recv()
@@ -263,23 +256,28 @@
     for k in range(NX):
         gpart[k] = gram[k * CHUNK : (k + 1) * CHUNK, :]
 
+    def batch(ref, count, n):
+        return pltpu.make_async_remote_copy(
+            src_ref=ref.at[pl.ds(0, count)], dst_ref=ref.at[pl.ds(0, count)], send_sem=gsem.at[n], recv_sem=gsem.at[n + 1],
+            device_id={"col": sibling}, device_id_type=MESH,
+        )
+
     def x_scatter(d, sign):
         to = (x + sign * d + NX) % NX
         return pltpu.make_async_remote_copy(
-            src_ref=gpart.at[to], dst_ref=gx.at[x], send_sem=gs1.at[d], recv_sem=gr1.at[d],
+            src_ref=gpart.at[to], dst_ref=gx.at[x], send_sem=gsem.at[0], recv_sem=gsem.at[1],
             device_id={"dom": to * NZ + z}, device_id_type=MESH,
         )
 
     for d in range(1, NX):
         x_scatter(d, 1).start()
     gx[x] = gpart[x]
-    for d in range(1, NX):
-        x_scatter(d, -1).wait_recv()
+    batch(gx, NX - 1, 0).wait_recv()
     gz[z] = ((gx[0] + gx[1]) + gx[2]) + gx[3]
 
     def z_share(owner, d):
         return pltpu.make_async_remote_copy(
-            src_ref=gz.at[owner], dst_ref=gz.at[owner], send_sem=gs2.at[d], recv_sem=gr2.at[d],
+            src_ref=gz.at[owner], dst_ref=gz.at[owner], send_sem=gsem.at[2], recv_sem=gsem.at[3],
             device_id={"dom": x * NZ + (z + d) % NZ}, device_id_type=MESH,
         )
 
@@ -292,8 +290,7 @@
         out_ref[:, cols] = jnp.dot(rot[...], whole[:, cols], preferred_element_type=jnp.float32).astype(jnp.bfloat16)
 
     loop(0, ROWS // 512, rotate)
-    for d in z_order:
-        z_share((z + NZ - d) % NZ, d).wait_recv()
+    batch(gz, NZ - 1, 2).wait_recv()
     total = gz[0]
     for k in range(1, NZ):
         total = total + gz[k]
@@ -301,7 +298,7 @@
 
     def x_share(owner, d):
         return pltpu.make_async_remote_copy(
-            src_ref=gsum.at[owner], dst_ref=gsum.at[owner], send_sem=gs3.at[d], recv_sem=gr3.at[d],
+            src_ref=gsum.at[owner], dst_ref=gsum.at[owner], send_sem=gsem.at[4], recv_sem=gsem.at[5],
             device_id={"dom": ((x + d) % NX) * NZ + z}, device_id_type=MESH,
         )
 
@@ -309,19 +306,19 @@
         x_share(x, d).start()
     for p in range(2):
         for h in range(HALVES):
-            send_ended(p, h)
-    for copy in sent:
-        copy.wait_send()
-    for d in range(1, NX):
-        x_scatter(d, 1).wait_send()
-    for d in range(1, NZ):
-        z_share(z, d).wait_send()
-    for d in range(1, NX):
-        x_share((x + NX - d) % NX, d).wait_recv()
+            halo_batch(p, h, 0, 0, NDOM - 1).wait_send()
+    for h in range(HALVES):
+        seven = whole.at[pl.ds(0, (2 * NY - 1) * PART)]
+        pltpu.make_async_remote_copy(
+            src_ref=seven, dst_ref=seven, send_sem=csend.at[h], recv_sem=crecv.at[h, 0],
+            device_id={"col": sibling}, device_id_type=MESH,
+        ).wait_send()
+    batch(gx, NX - 1, 0).wait_send()
+    batch(gz, NZ - 1, 2).wait_send()
+    batch(gsum, NX - 1, 4).wait_recv()
     for k in range(NX):
         gram_ref[k * CHUNK : (k + 1) * CHUNK, :] = gsum[k]
-    for d in range(1, NX):
-        x_share(x, d).wait_send()
+    batch(gsum, NX - 1, 4).wait_send()
 
 
 def per_device(tiles, tile_rows, tile_srcs, send_rows, basis, rotation):
@@ -356,16 +353,11 @@
             pltpu.VMEM((NX, CHUNK, K), jnp.float32),
             pltpu.VMEM((NZ, CHUNK, K), jnp.float32),
             dma((7,)),
-            dma((2, HALVES, NDOM)),
-            dma((2, HALVES, NDOM)),
+            dma((2, HALVES)),
+            dma((2, HALVES, HALF)),
+            dma((HALVES,)),
             dma((HALVES, 2 * NY)),
-            dma((HALVES, 2 * NY)),
-            dma((NX,)),
-            dma((NX,)),
-            dma((NZ,)),
-            dma((NZ,)),
-            dma((NX,)),
-            dma((NX,)),
+            dma((6,)),
         ],
         compiler_params=pltpu.CompilerParams(collective_id=0, has_side_effects=True, vmem_limit_bytes=56 << 20),
         cost_estimate=pl.CostEstimate(flops=300_000_000, bytes_accessed=4 << 20, transcendentals=0),

time: 98.1 us -> 93.3 us (0.951)
  Pallas kernels: 94.3 us -> 89.5 us
    pallas_call x1, Pallas kernels: 94.3 us -> 89.5 us  [per_device(): pl.pallas_call(kernel, out_shape=(jax.ShapeDtypeStruct((WIDTH, K), jnp.fl...]
where the time goes in v3:
time: 93.3 us; the launch traced here: 93.1 us
  Pallas kernels  89.5 us (96%)
  local copies, waits for them, and re-layouts  2.94 us (3%)
    pallas_call x1, Pallas kernels, per_device(): pl.pallas_call(kernel, out_shape=(jax.ShapeDtypeStruct((WIDTH, K), jnp.fl...  89.5 us
    unnamed x2, local copies, waits for them, and re-layouts  2.94 us

profile of v3, /device:TPU:1, one launch (start us, length us, event | category | flops | bytes accessed | tf_op | source)
XLA Modules:
  0.0 93.1 jit_solution(10529350730790595021)
XLA Ops:
  0.6 89.5 %shard_map.77 = (f32[32,256]{1,0:T(8,128)}, bf16[32,2048]{1,0:T(8,128)(2,1)}) custom-call(bf16[96,128,128]{2,1,0:T(8,128)(2,1)} %tiles_h.1, s32[1,96]{1,0:T(1,128)} %bitcast.6, s32[1,96]{1,0:T(1,128)} %bitcast.7, s32[1,64]{1,0:T(1,128)} %send_h.1, bf16[32,2048]{1,0:T(8,128)(2,1)} %basis_h.1, bf16[32,256]{1,0:T(8,128)(2,1)} %bitcast.5), custom_call_target="tpu_custom_call" | custom-call | flops 300000000 | bytes 4194304 | tf_op jit(solution)/shard_map/pallas_call | solution.py:328
  90.2 1.4 %copy.10 = f32[256,32]{0,1:T(8,128)} copy(f32[256,32]{0,1:T(8,128)} %bitcast.4) | data formatting | bytes 65536
  91.5 1.6 %copy.11 = bf16[32,2048]{1,0:T(8,128)(2,1)} copy(bf16[32,2048]{1,0:T(8,128)(2,1)} %get-tuple-element.9) | data formatting | bytes 262144

commit v4 on v3

--- a/solution.py
+++ b/solution.py
@@ -273,7 +273,8 @@
         x_scatter(d, 1).start()
     gx[x] = gpart[x]
     batch(gx, NX - 1, 0).wait_recv()
-    gz[z] = ((gx[0] + gx[1]) + gx[2]) + gx[3]
+    mine_x = ((gx[0] + gx[1]) + gx[2]) + gx[3]
+    gz[z] = jnp.concatenate([mine_x[:, 0:TILE], mine_x[:, TILE:K]], axis=0).astype(jnp.bfloat16)
 
     def z_share(owner, d):
         return pltpu.make_async_remote_copy(
@@ -291,10 +292,10 @@
 
     loop(0, ROWS // 512, rotate)
     batch(gz, NZ - 1, 2).wait_recv()
-    total = gz[0]
+    total = gz[0].astype(jnp.float32)
     for k in range(1, NZ):
-        total = total + gz[k]
-    gsum[x] = total
+        total = total + gz[k].astype(jnp.float32)
+    gsum[x] = jnp.concatenate([total[0:CHUNK], total[CHUNK:]], axis=1)
 
     def x_share(owner, d):
         return pltpu.make_async_remote_copy(
@@ -328,8 +329,8 @@
     gram, rotated = pl.pallas_call(
         kernel,
         out_shape=(
-            jax.ShapeDtypeStruct((WIDTH, K), jnp.float32),
-            jax.ShapeDtypeStruct((WIDTH, ROWS), jnp.bfloat16),
+            pltpu.VMEM((WIDTH, K), jnp.float32),
+            pltpu.VMEM((WIDTH, ROWS), jnp.bfloat16),
         ),
         in_specs=[any_space] * 6,
         out_specs=(vmem, vmem),
@@ -351,7 +352,7 @@
             pltpu.VMEM((NX, CHUNK, K), jnp.float32),
             pltpu.VMEM((NX, CHUNK, K), jnp.float32),
             pltpu.VMEM((NX, CHUNK, K), jnp.float32),
-            pltpu.VMEM((NZ, CHUNK, K), jnp.float32),
+            pltpu.VMEM((NZ, 2 * CHUNK, TILE), jnp.bfloat16),
             dma((7,)),
             dma((2, HALVES)),
             dma((2, HALVES, HALF)),

time: 93.3 us -> 88.9 us (0.953)
  Pallas kernels: 89.5 us -> 86.8 us
  local copies, waits for them, and re-layouts: 2.94 us -> 1.27 us
    pallas_call x1, Pallas kernels: 89.5 us -> 86.8 us  [per_device(): pl.pallas_call(kernel, out_shape=(pltpu.VMEM((WIDTH, K), jnp.float32), pl...]
    unnamed x2, local copies, waits for them, and re-layouts: 2.94 us -> 1.27 us
where the time goes in v4:
time: 88.9 us; the launch traced here: 88.7 us
  Pallas kernels  86.8 us (98%)
  local copies, waits for them, and re-layouts  1.27 us (1%)
    pallas_call x1, Pallas kernels, per_device(): pl.pallas_call(kernel, out_shape=(pltpu.VMEM((WIDTH, K), jnp.float32), pl...  86.8 us

profile of v4, /device:TPU:1, one launch (start us, length us, event | category | flops | bytes accessed | tf_op | source)
XLA Modules:
  0.0 88.7 jit_solution(15165659447245355511)
XLA Ops:
  0.6 86.8 %shard_map.77 = (f32[32,256]{1,0:T(8,128)S(1)}, bf16[32,2048]{1,0:T(8,128)(2,1)S(1)}) custom-call(bf16[96,128,128]{2,1,0:T(8,128)(2,1)} %tiles_h.1, s32[1,96]{1,0:T(1,128)} %bitcast.6, s32[1,96]{1,0:T(1,128)} %bitcast.7, s32[1,64]{1,0:T(1,128)} %send_h.1, bf16[32,2048]{1,0:T(8,128)(2,1)} %basis_h.1, bf16[32,256]{1,0:T(8,128)(2,1)} %bitcast.5), custom_call_target="tpu_custom_call" | custom-call | flops 300000000 | bytes 4194304 | tf_op jit(solution)/shard_map/pallas_call | solution.py:329
  87.4 0.6 copy.10
  88.0 0.7 copy.11

commit v5 on v4

--- a/solution.py
+++ b/solution.py
@@ -20,6 +20,7 @@
 GROUP = 4
 HALF = NZ // 2
 BATCH = 2 * NX
+REACH = 3
 HALVES = 2
 PART = WIDTH // HALVES
 CHUNK = WIDTH // NX
@@ -73,9 +74,9 @@
     tiles_h, rows_h, srcs_h, send_h, basis_h, rot_h,
     gram_ref, out_ref,
     tiles, rows, srcs, send_rows, basis, rot, tab, tabs,
-    field, sbuf, rbuf, prods, sums, whole,
+    field, lent_refs, lent_rows, lent_list, sbuf, rbuf, prods, sums, whole,
     gpart, gx, gsum, gz,
-    in_sem, ssem, rsem, csend, crecv, gsem,
+    in_sem, fsend, frecv, lsend, lrecv, ssem, rsem, csend, crecv, gsem,
 ):
     me, mc = lax.axis_index("dom"), lax.axis_index("col")
     x, z = lax.div(me, NZ), lax.rem(me, NZ)
@@ -94,6 +95,7 @@
     def over_peers(body):
         loop(0, HALF - 1, lambda j: body(j, BATCH))
         body(HALF - 1, BATCH - 1)
+    lent = [[[lent_refs[(p * HALVES + h) * 2 + side] for side in range(2)] for h in range(HALVES)] for p in range(2)]
     bar = pltpu.get_barrier_semaphore()
 
     loads = [
@@ -126,7 +128,7 @@
         loads[n].wait()
     for h in range(HALVES):
         for r in range(RB):
-            field[h, r] = basis[h * PART : (h + 1) * PART, r * TILE : (r + 1) * TILE]
+            field[0, h, r] = basis[h * PART : (h + 1) * PART, r * TILE : (r + 1) * TILE]
 
     pl.semaphore_wait(bar, NDOM - 1 + NY)
 
@@ -147,22 +149,71 @@
     def product(block, tile):
         return lax.dot_general(block, tile, (((1,), (1,)), ((), ())), preferred_element_type=jnp.float32)
 
+    def along_z(d):
+        return lax.rem(z + (d + NZ), NZ)
+
+    def whole_field(p, h, side):
+        to = along_z(REACH if side == 0 else -REACH)
+        return pltpu.make_async_remote_copy(
+            src_ref=field.at[p, h], dst_ref=lent[p][h][side], send_sem=fsend.at[p, h, side], recv_sem=frecv.at[p, h, side],
+            device_id={"dom": x * NZ + to}, device_id_type=MESH,
+        )
+
+    def lists(side):
+        to = along_z(REACH if side == 0 else -REACH)
+        return pltpu.make_async_remote_copy(
+            src_ref=send_h, dst_ref=lent_rows.at[side], send_sem=lsend.at[side], recv_sem=lrecv.at[side],
+            device_id={"dom": x * NZ + to}, device_id_type=MESH,
+        )
+
+    def place_of(side, far):
+        return (HALF - 1 - far, NX) if side == 0 else (HALF - far, 0)
+
     def send(p, h):
-        def some(j, most):
-            peers = targets(j)
-            for u, peer in enumerate(peers[:most]):
-                sbuf[p, h, j * BATCH + u] = field[h, send_rows[0, peer]]
-            for u, peer in enumerate(peers[:most]):
+        for side in range(2):
+            whole_field(p, h, side).start()
+        near = []
+        for side in range(2):
+            j, first = place_of(side, 1)
+            to = along_z(1 if side == 0 else -1)
+            near += [(j, first + NX - 1 - dx, lines_to[dx] + to) for dx in range(NX)]
+        near += [(HALF - 1, BATCH - 1 - dx, lines_to[dx] + z) for dx in range(1, NX)]
+        for j, u, peer in near:
+            sbuf[p, h, j * BATCH + u] = field[p, h, send_rows[0, peer]]
+        for j, u, peer in near:
+            halo(p, h, j, u, peer).start()
+        rbuf[p, h, NDOM - 1] = field[p, h, send_rows[0, me]]
+
+    def hand_on(p, h):
+        for side in range(2):
+            whole_field(p, h, side).wait_recv()
+
+            def some(far, chosen=range(NX), side=side):
+                j, first = place_of(side, far)
+                to = along_z(far - REACH) if side == 0 else along_z(REACH - far)
+                all_of = [(first + NX - 1 - dx, lines_to[dx] + to) for dx in chosen]
+                for u, peer in all_of:
+                    sbuf[p, h, j * BATCH + u] = lent[p][h][side][lent_list[side, 0, peer]]
+                for u, peer in all_of:
+                    halo(p, h, j, u, peer).start()
+
+            j, to = 0, along_z(HALF - REACH) if side == 0 else along_z(REACH - HALF)
+            halfway = [(NX - 1 - dx, lines_to[dx] + to) for dx in ((3, 2) if side == 0 else (1, 0))]
+            for u, peer in halfway:
+                sbuf[p, h, u] = lent[p][h][side][lent_list[side, 0, peer]]
+            for u, peer in halfway:
                 halo(p, h, j, u, peer).start()
-
-        over_peers(some)
-        rbuf[p, h, NDOM - 1] = field[h, send_rows[0, me]]
-
-    def own(h):
+            loop(0, HALF - 1 - REACH, lambda k, some=some: some(HALF - 1 - k))
+            some(REACH - 1)
+            some(REACH, range(1, NX))
+            j, first = place_of(side, REACH)
+            rbuf[p, h, j * BATCH + first + NX - 1] = lent[p][h][side][lent_list[side, 0, me]]
+
+    def own(p, h):
         def group(g):
             for u in range(GROUP):
                 s = NDOM + g * GROUP + u
-                prods[h, s] = product(field[h, tabs[1, s]], tiles[tabs[0, s]])
+                prods[h, s] = product(field[p, h, tabs[1, s]], tiles[tabs[0, s]])
 
         loop(0, OWN // GROUP, group)
 
@@ -172,9 +223,12 @@
             for u, peer in enumerate(origins(j)):
                 prods[h, peer] = product(rbuf[p, h, j * BATCH + u], tiles[tabs[0, peer]])
 
-        loop(first, min(past, HALF - 1), lambda j: take(j, BATCH))
-        if past == HALF:
-            take(HALF - 1, BATCH - 1)
+        edge = place_of(1, REACH)[0] + 1
+        for j in range(HALF - 1, edge - 3, -1):
+            if first <= HALF - 1 - j < past:
+                take(j, BATCH - (j in (HALF - 1, edge - 1, edge - 2)))
+        lo = max(first, HALF - edge + 2)
+        loop(lo, past, lambda k: take(HALF - 1 - k, BATCH))
 
     def add_up(h):
         def running(g, acc):
@@ -214,13 +268,15 @@
 
     def first_done(h):
         for r, block in enumerate(add_up(h)):
-            field[h, r] = block
+            field[1, h, r] = block
 
     def second_done(h):
         mine = pl.ds(pl.multiple_of(mc * WIDTH + h * PART, PART), PART)
         for r, block in enumerate(add_up(h)):
             whole[mine, r * TILE : (r + 1) * TILE] = block
 
+    for side in range(2):
+        lists(side).start()
     for h in range(HALVES):
         send(0, h)
     for n in range(2, 5):
@@ -229,13 +285,23 @@
     to_smem = pltpu.make_async_copy(tab, tabs, in_sem.at[6])
     to_smem.start()
     to_smem.wait()
-    for h in range(HALVES):
-        own(h)
+    for side in range(2):
+        lists(side).wait_recv()
+    lists_in = pltpu.make_async_copy(lent_rows, lent_list, in_sem.at[7])
+    lists_in.start()
+    lists_in.wait()
+    for h in range(HALVES):
+        hand_on(0, h)
+        own(0, h)
     for h in range(HALVES):
         receive(0, h, 0, HALF)
         first_done(h)
         send(1, h)
-        own(h)
+        if h < HALVES - 1:
+            own(1, h)
+    for h in range(HALVES):
+        hand_on(1, h)
+    own(1, HALVES - 1)
     for h in range(HALVES):
         receive(1, h, 0, HALF - 2)
         if h > 0:
@@ -307,7 +373,11 @@
         x_share(x, d).start()
     for p in range(2):
         for h in range(HALVES):
-            halo_batch(p, h, 0, 0, NDOM - 1).wait_send()
+            halo_batch(p, h, 0, 0, NDOM - 3).wait_send()
+            for side in range(2):
+                whole_field(p, h, side).wait_send()
+    for side in range(2):
+        lists(side).wait_send()
     for h in range(HALVES):
         seven = whole.at[pl.ds(0, (2 * NY - 1) * PART)]
         pltpu.make_async_remote_copy(
@@ -343,7 +413,10 @@
             pltpu.VMEM((WIDTH, K), jnp.bfloat16),
             pltpu.VMEM((8, 128), jnp.int32),
             pltpu.SMEM((8, 128), jnp.int32),
-            pltpu.VMEM((HALVES, RB, PART, TILE), jnp.bfloat16),
+            pltpu.VMEM((2, HALVES, RB, PART, TILE), jnp.bfloat16),
+            [pltpu.VMEM((RB, PART, TILE), jnp.bfloat16)] * (4 * HALVES),
+            pltpu.VMEM((2, 1, NDOM), jnp.int32),
+            pltpu.SMEM((2, 1, NDOM), jnp.int32),
             pltpu.VMEM((2, HALVES, NDOM, PART, TILE), jnp.bfloat16),
             pltpu.VMEM((2, HALVES, NDOM, PART, TILE), jnp.bfloat16),
             pltpu.VMEM((HALVES, TPD, PART, TILE), jnp.float32),
@@ -353,7 +426,11 @@
             pltpu.VMEM((NX, CHUNK, K), jnp.float32),
             pltpu.VMEM((NX, CHUNK, K), jnp.float32),
             pltpu.VMEM((NZ, 2 * CHUNK, TILE), jnp.bfloat16),
-            dma((7,)),
+            dma((8,)),
+            dma((2, HALVES, 2)),
+            dma((2, HALVES, 2)),
+            dma((2,)),
+            dma((2,)),
             dma((2, HALVES)),
             dma((2, HALVES, HALF)),
             dma((HALVES,)),

time: 88.9 us -> 86.4 us (0.972)
  Pallas kernels: 86.8 us -> 84.4 us
    pallas_call x1, Pallas kernels: 86.8 us -> 84.4 us  [per_device(): pl.pallas_call(kernel, out_shape=(pltpu.VMEM((WIDTH, K), jnp.float32), pl...]
where the time goes in v5:
time: 86.4 us; the launch traced here: 86.3 us
  Pallas kernels  84.4 us (98%)
  local copies, waits for them, and re-layouts  1.27 us (1%)
    pallas_call x1, Pallas kernels, per_device(): pl.pallas_call(kernel, out_shape=(pltpu.VMEM((WIDTH, K), jnp.float32), pl...  84.4 us

profile of v5, /device:TPU:1, one launch (start us, length us, event | category | flops | bytes accessed | tf_op | source)
XLA Modules:
  0.0 86.3 jit_solution(16998209520428944794)
XLA Ops:
  0.6 84.4 %shard_map.77 = (f32[32,256]{1,0:T(8,128)S(1)}, bf16[32,2048]{1,0:T(8,128)(2,1)S(1)}) custom-call(bf16[96,128,128]{2,1,0:T(8,128)(2,1)} %tiles_h.1, s32[1,96]{1,0:T(1,128)} %bitcast.6, s32[1,96]{1,0:T(1,128)} %bitcast.7, s32[1,64]{1,0:T(1,128)} %send_h.1, bf16[32,2048]{1,0:T(8,128)(2,1)} %basis_h.1, bf16[32,256]{1,0:T(8,128)(2,1)} %bitcast.5), custom_call_target="tpu_custom_call" | custom-call | flops 300000000 | bytes 4194304 | tf_op jit(solution)/shard_map/pallas_call | solution.py:399
  85.0 0.6 copy.10
  85.6 0.7 copy.11

commit v6 on v5

--- a/solution.py
+++ b/solution.py
@@ -285,6 +285,8 @@
     to_smem = pltpu.make_async_copy(tab, tabs, in_sem.at[6])
     to_smem.start()
     to_smem.wait()
+    for h in range(HALVES):
+        own(0, h)
     for side in range(2):
         lists(side).wait_recv()
     lists_in = pltpu.make_async_copy(lent_rows, lent_list, in_sem.at[7])
@@ -292,7 +294,6 @@
     lists_in.wait()
     for h in range(HALVES):
         hand_on(0, h)
-        own(0, h)
     for h in range(HALVES):
         receive(0, h, 0, HALF)
         first_done(h)

time: 86.4 us -> 86.1 us (level)
  no operation moved by 1% of the time
where the time goes in v6:
time: 86.1 us; the launch traced here: 85.5 us
  Pallas kernels  83.6 us (97%)
  local copies, waits for them, and re-layouts  1.27 us (1%)
    pallas_call x1, Pallas kernels, per_device(): pl.pallas_call(kernel, out_shape=(pltpu.VMEM((WIDTH, K), jnp.float32), pl...  83.6 us

profile of v6, /device:TPU:1, one launch (start us, length us, event | category | flops | bytes accessed | tf_op | source)
XLA Modules:
  0.0 85.5 jit_solution(11262615899920603883)
XLA Ops:
  0.6 83.6 %shard_map.77 = (f32[32,256]{1,0:T(8,128)S(1)}, bf16[32,2048]{1,0:T(8,128)(2,1)S(1)}) custom-call(bf16[96,128,128]{2,1,0:T(8,128)(2,1)} %tiles_h.1, s32[1,96]{1,0:T(1,128)} %bitcast.6, s32[1,96]{1,0:T(1,128)} %bitcast.7, s32[1,64]{1,0:T(1,128)} %send_h.1, bf16[32,2048]{1,0:T(8,128)(2,1)} %basis_h.1, bf16[32,256]{1,0:T(8,128)(2,1)} %bitcast.5), custom_call_target="tpu_custom_call" | custom-call | flops 300000000 | bytes 4194304 | tf_op jit(solution)/shard_map/pallas_call | solution.py:400
  84.2 0.6 copy.10
  84.9 0.7 copy.11
